TPU v7x, 512 devices: a whole 4x4x16 slice. The times are simulated.
512 devices in a mesh: cp: 64 (over z, y), hd: 8 (over x, core).
Axes of the slice: x: 4, y: 4, z: 16, core: 2. Of those that a mesh axis runs over, the one named last changes fastest.
Arguments:
- queries: bfloat16 [32768, 4096], P(('cp', 'hd')), may hold values from -10 to 10
- keys: bfloat16 [32768, 1024], P(('cp', 'hd')), may hold values from -10 to 10
- values: bfloat16 [32768, 1024], P(('cp', 'hd')), may hold values from -6 to 6
- doc_starts: int32 [16], replicated, may hold values from 0 to 28672, as said below
Outputs:
- attended: bfloat16 [32768, 4096], P(('cp', 'hd'))
Inputs may be any that keep to these rules, and one draw needn't show every extreme that they name: `doc_starts`: offsets rise strictly from 0; every document holds 512 to 4096 tokens; the last document holds 4096 tokens and ends at 32768.
All inputs are finite; a program needn't handle non-finite values.
Results may differ from a plain program's by a relative error of at most 0.014.
Values may be sent and summed in bfloat16 or wider, within the bound.
No kernel may reach another device: no remote copies, remote signals or barrier semaphores. Data moves between devices by JAX's collectives and lax.ppermute only.
A program may use at most 64 MiB of HBM per device.

v0:
```python
import jax
import jax.numpy as jnp
from jax import lax
from jax.sharding import PartitionSpec as P

D_HEAD = 128
BLOCK = 512
MAX_DOC = 4096


FLOOR = -1e30


def from_behind(block, axis, distance):
    devices = range(lax.axis_size(axis))
    route = [(i - distance, i) for i in devices if i - distance in devices]
    return lax.ppermute(block, axis, route)


def doc_number(doc_starts, position):
    return jnp.sum((doc_starts <= position).astype(jnp.int32)) - 1


def doc_rows(doc_starts, positions):
    return jnp.sum((doc_starts[None, :] <= positions[:, None]).astype(jnp.int32), axis=1) - 1


def empty_state(kv_local, group_size, row_count):
    maxima = jnp.full((kv_local, group_size, row_count), FLOOR, jnp.float32)
    totals = jnp.zeros((kv_local, group_size, row_count), jnp.float32)
    accumulated = jnp.zeros((kv_local, group_size, row_count, D_HEAD), jnp.float32)
    return (maxima, totals, accumulated)


def fold_piece(state, query, q_first, pair_kv, k_first, doc_starts):
    keys_part, values_part = pair_kv
    block_count = query.shape[0] // BLOCK
    score_scale = D_HEAD ** (-0.5)

    def visit_pair(pair_index, running):
        q_block = pair_index // block_count
        k_block = pair_index % block_count
        q_start = q_first + q_block * BLOCK
        k_start = k_first + k_block * BLOCK
        nonempty = (k_start >= 0) & (k_start <= q_start)
        nonempty = nonempty & (
            doc_number(doc_starts, k_start + BLOCK - 1) >= doc_number(doc_starts, q_start)
        )

        def attend(running):
            maxima, totals, accumulated = running
            q_pos = q_start + jnp.arange(BLOCK, dtype=jnp.int32)
            k_pos = k_start + jnp.arange(BLOCK, dtype=jnp.int32)
            allowed = doc_rows(doc_starts, q_pos)[:, None] == doc_rows(doc_starts, k_pos)[None, :]
            allowed = allowed & (k_pos[None, :] <= q_pos[:, None])
            scores = (
                jnp.einsum("qhgd,khd->hgqk", query, keys_part, preferred_element_type=jnp.float32)
                * score_scale
            )
            old_max = maxima
            old_total = totals
            old_accum = accumulated
            new_max = jnp.maximum(old_max, jnp.max(jnp.where(allowed, scores, FLOOR), axis=3))
            weights = jnp.where(allowed, jnp.exp(scores - new_max[..., None]), 0.0)
            rescale = jnp.exp(old_max - new_max)
            new_total = old_total * rescale + jnp.sum(weights, axis=3)
            product = jnp.einsum(
                "hgqk,khd->hgqd",
                weights.astype(jnp.bfloat16),
                values_part,
                preferred_element_type=jnp.float32,
            )
            new_accum = old_accum * rescale[..., None] + product
            maxima = new_max
            totals = new_total
            accumulated = new_accum
            return (maxima, totals, accumulated)

        return lax.cond(nonempty, attend, lambda kept: kept, running)

    return lax.fori_loop(0, block_count * block_count, visit_pair, state)


def per_device(queries, keys, values, doc_starts):
    heads_q, heads_k, heads_v = (
        lax.all_to_all(queries, "hd", split_axis=1, concat_axis=0, tiled=True),
        lax.all_to_all(keys, "hd", split_axis=1, concat_axis=0, tiled=True),
        lax.all_to_all(values, "hd", split_axis=1, concat_axis=0, tiled=True),
    )
    row_count = heads_q.shape[0]
    kv_local = heads_k.shape[1] // D_HEAD
    group_size = heads_q.shape[1] // heads_k.shape[1]
    query = heads_q.reshape(row_count, kv_local, group_size, D_HEAD)
    own_kv = (
        heads_k.reshape(row_count, kv_local, D_HEAD),
        heads_v.reshape(row_count, kv_local, D_HEAD),
    )
    device = lax.axis_index("cp")
    first_row = device * row_count
    reach_devices = (MAX_DOC + row_count - 2) // row_count
    state = fold_piece(
        empty_state(kv_local, group_size, row_count),
        query,
        first_row,
        own_kv,
        first_row,
        doc_starts,
    )
    for distance in range(1, reach_devices + 1):
        arrived = from_behind((own_kv[0], own_kv[1]), "cp", distance)
        state = fold_piece(
            state, query, first_row, arrived, first_row - distance * row_count, doc_starts
        )
    maxima, totals, accumulated = state
    result = accumulated / totals[..., None]
    result = (
        jnp.transpose(result, (2, 0, 1, 3))
        .reshape(row_count, kv_local * group_size * D_HEAD)
        .astype(jnp.bfloat16)
    )
    return lax.all_to_all(result, "hd", split_axis=0, concat_axis=1, tiled=True)


def solution(mesh):
    in_specs = (P(("cp", "hd"), None), P(("cp", "hd"), None), P(("cp", "hd"), None), P())
    out_specs = P(("cp", "hd"), None)
    return jax.shard_map(
        per_device, mesh=mesh, in_specs=in_specs, out_specs=out_specs, check_vma=False
    )
```

profile of v0, /device:TPU:160, one launch (start us, length us, event | category | flops | bytes accessed | tf_op | source)
XLA Modules:
  0.0 146.5 jit_solution(14830859043840624974)
XLA Ops:
  1.6 4.3 %all-to-all-start = ((bf16[64,8,128]{2,0,1:T(8,128)(2,1)}), bf16[64,8,128]{2,0,1:T(8,128)(2,1)}, u32[]{:S(2)}, u32[]{:S(2)}) async-start(bf16[64,8,128]{2,0,1:T(8,128)(2,1)} %copy_bitcast_fusion.2), calls=%async_computation | async-start | bytes 262144 | tf_op jit(solution)/shard_map/all_to_all | solution.py:87
  7.5 4.7 %all-to-all-done = bf16[64,8,128]{2,0,1:T(8,128)(2,1)} async-done(((bf16[64,8,128]{2,0,1:T(8,128)(2,1)}), bf16[64,8,128]{2,0,1:T(8,128)(2,1)}, u32[]{:S(2)}, u32[]{:S(2)}) %all-to-all-start) | async-done | bytes 131104 | tf_op jit(solution)/shard_map/all_to_all | solution.py:87
  12.1 4.0 %all-to-all-start.2 = ((bf16[64,8,128]{2,0,1:T(8,128)(2,1)}), bf16[64,8,128]{2,0,1:T(8,128)(2,1)}, u32[]{:S(2)}, u32[]{:S(2)}) async-start(bf16[64,8,128]{2,0,1:T(8,128)(2,1)} %copy_bitcast_fusion.1), calls=%async_computation.2 | async-start | bytes 262144 | tf_op jit(solution)/shard_map/all_to_all | solution.py:88
  16.1 3.5 %collective-permute-start = (bf16[512,1,128]{2,0,1:T(8,128)(2,1)}, bf16[512,1,128]{2,0,1:T(8,128)(2,1)S(1)}, u32[]{:S(2)}, u32[]{:S(2)}) collective-permute-start(bf16[512,1,128]{2,0,1:T(8,128)(2,1)} %bitcast.127), channel_id=1, source_target_pairs={{0,8},{8,16},{16,24},{24,32},{32,40},{40,48},{48,56},{56,64},{64,7... | collective-permute-start | bytes 393224 | tf_op jit(solution)/shard_map/ppermute | solution.py:17
  22.3 3.9 %all-to-all-start.1 = ((bf16[64,8,512]{2,0,1:T(8,128)(2,1)}), bf16[64,8,512]{2,0,1:T(8,128)(2,1)S(1)}, u32[]{:S(2)}, u32[]{:S(2)}) async-start(bf16[64,8,512]{2,0,1:T(8,128)(2,1)} %bitcast.540), calls=%async_computation.1 | async-start | bytes 1048576 | tf_op jit(solution)/shard_map/all_to_all | solution.py:86
  26.2 3.5 %collective-permute-start.1 = (bf16[512,1,128]{2,0,1:T(8,128)(2,1)}, bf16[512,1,128]{2,0,1:T(8,128)(2,1)S(1)}, u32[]{:S(2)}, u32[]{:S(2)}) collective-permute-start(bf16[512,1,128]{2,0,1:T(8,128)(2,1)} %bitcast.130), channel_id=1, source_target_pairs={{0,8},{8,16},{16,24},{24,32},{32,40},{40,48},{48,56},{56,64},{64,7... | collective-permute-start | bytes 393224 | tf_op jit(solution)/shard_map/ppermute | solution.py:17
  29.7 4.8 %collective-permute-start.2 = (bf16[512,1,128]{2,0,1:T(8,128)(2,1)}, bf16[512,1,128]{2,0,1:T(8,128)(2,1)S(1)}, u32[]{:S(2)}, u32[]{:S(2)}) collective-permute-start(bf16[512,1,128]{2,0,1:T(8,128)(2,1)} %bitcast.127), channel_id=1, source_target_pairs={{0,16},{8,24},{16,32},{24,40},{32,48},{40,56},{48,64},{56,72},{64,... | collective-permute-start | bytes 393224 | tf_op jit(solution)/shard_map/ppermute | solution.py:17
  34.5 3.9 %collective-permute-start.3 = (bf16[512,1,128]{2,0,1:T(8,128)(2,1)}, bf16[512,1,128]{2,0,1:T(8,128)(2,1)S(1)}, u32[]{:S(2)}, u32[]{:S(2)}) collective-permute-start(bf16[512,1,128]{2,0,1:T(8,128)(2,1)} %bitcast.130), channel_id=1, source_target_pairs={{0,16},{8,24},{16,32},{24,40},{32,48},{40,56},{48,64},{56,72},{64,... | collective-permute-start | bytes 393224 | tf_op jit(solution)/shard_map/ppermute | solution.py:17
  38.4 4.9 %collective-permute-start.4 = (bf16[512,1,128]{2,0,1:T(8,128)(2,1)}, bf16[512,1,128]{2,0,1:T(8,128)(2,1)S(1)}, u32[]{:S(2)}, u32[]{:S(2)}) collective-permute-start(bf16[512,1,128]{2,0,1:T(8,128)(2,1)} %bitcast.127), channel_id=1, source_target_pairs={{0,24},{8,32},{16,40},{24,48},{32,56},{40,64},{48,72},{56,80},{64,... | collective-permute-start | bytes 393224 | tf_op jit(solution)/shard_map/ppermute | solution.py:17
  43.3 4.9 %collective-permute-start.5 = (bf16[512,1,128]{2,0,1:T(8,128)(2,1)}, bf16[512,1,128]{2,0,1:T(8,128)(2,1)S(1)}, u32[]{:S(2)}, u32[]{:S(2)}) collective-permute-start(bf16[512,1,128]{2,0,1:T(8,128)(2,1)} %bitcast.130), channel_id=1, source_target_pairs={{0,24},{8,32},{16,40},{24,48},{32,56},{40,64},{48,72},{56,80},{64,... | collective-permute-start | bytes 393224 | tf_op jit(solution)/shard_map/ppermute | solution.py:17
  48.3 3.4 %collective-permute-start.6 = (bf16[512,1,128]{2,0,1:T(8,128)(2,1)}, bf16[512,1,128]{2,0,1:T(8,128)(2,1)S(1)}, u32[]{:S(2)}, u32[]{:S(2)}) collective-permute-start(bf16[512,1,128]{2,0,1:T(8,128)(2,1)} %bitcast.127), channel_id=1, source_target_pairs={{0,32},{8,40},{16,48},{24,56},{32,64},{40,72},{48,80},{56,88},{64,... | collective-permute-start | bytes 393224 | tf_op jit(solution)/shard_map/ppermute | solution.py:17
  54.7 3.4 %collective-permute-start.8 = (bf16[512,1,128]{2,0,1:T(8,128)(2,1)}, bf16[512,1,128]{2,0,1:T(8,128)(2,1)S(1)}, u32[]{:S(2)}, u32[]{:S(2)}) collective-permute-start(bf16[512,1,128]{2,0,1:T(8,128)(2,1)} %bitcast.127), channel_id=1, source_target_pairs={{0,40},{8,48},{16,56},{24,64},{32,72},{40,80},{48,88},{56,96},{64,... | collective-permute-start | bytes 393224 | tf_op jit(solution)/shard_map/ppermute | solution.py:17
  60.9 6.1 %collective-permute-start.10 = (bf16[512,1,128]{2,0,1:T(8,128)(2,1)}, bf16[512,1,128]{2,0,1:T(8,128)(2,1)S(1)}, u32[]{:S(2)}, u32[]{:S(2)}) collective-permute-start(bf16[512,1,128]{2,0,1:T(8,128)(2,1)} %bitcast.127), channel_id=1, source_target_pairs={{0,48},{8,56},{16,64},{24,72},{32,80},{40,88},{48,96},{56,104},{64... | collective-permute-start | bytes 393224 | tf_op jit(solution)/shard_map/ppermute | solution.py:17
  69.7 4.2 %collective-permute-start.12 = (bf16[512,1,128]{2,0,1:T(8,128)(2,1)}, bf16[512,1,128]{2,0,1:T(8,128)(2,1)S(1)}, u32[]{:S(2)}, u32[]{:S(2)}) collective-permute-start(bf16[512,1,128]{2,0,1:T(8,128)(2,1)} %bitcast.127), channel_id=1, source_target_pairs={{0,56},{8,64},{16,72},{24,80},{32,88},{40,96},{48,104},{56,112},{6... | collective-permute-start | bytes 393224 | tf_op jit(solution)/shard_map/ppermute | solution.py:17
  90.6 5.6 %conditional.9 = ((f32[1,4,512]{2,1,0:T(4,128)S(1)}, f32[1,4,512]{2,1,0:T(4,128)S(1)}, f32[1,4,512,128]{3,2,1,0:T(8,128)S(1)})) conditional(s32[]{:T(128)} %convert_element_type.204, (f32[1,4,512]{2,1,0:T(4,128)S(1)}, f32[1,4,512]{2,1,0:T(4,128)S(1)}, f32[1,4,512,128]{3,2,1,0:T(8,128)S(1)}) %tuple.84, (s32[16]{0:T(128)S(1)}, s32[]{:T(128)}, ...), branch_computations={%region_10.11_spmd, %region_11.0_spmd} | conditional | flops 549747200 | bytes 16660580 | solution.py:79
  96.3 3.8 %conditional.10 = ((f32[1,4,512]{2,1,0:T(4,128)S(1)}, f32[1,4,512]{2,1,0:T(4,128)S(1)}, f32[1,4,512,128]{3,2,1,0:T(8,128)S(1)})) conditional(s32[]{:T(128)} %convert_element_type.202, (f32[1,4,512]{2,1,0:T(4,128)S(1)}, f32[1,4,512]{2,1,0:T(4,128)S(1)}, f32[1,4,512,128]{3,2,1,0:T(8,128)S(1)}) %get-tuple-element.1032, (s32[16]{0:T(128)S(1)}, ...), branch_computations={%region_16.17_spmd, %region_17.22_spmd} | conditional | flops 549772288 | bytes 16674920 | solution.py:79
  100.1 4.0 %conditional.11 = ((f32[1,4,512]{2,1,0:T(4,128)S(1)}, f32[1,4,512]{2,1,0:T(4,128)S(1)}, f32[1,4,512,128]{3,2,1,0:T(8,128)S(1)})) conditional(s32[]{:T(128)} %convert_element_type.200, (f32[1,4,512]{2,1,0:T(4,128)S(1)}, f32[1,4,512]{2,1,0:T(4,128)S(1)}, f32[1,4,512,128]{3,2,1,0:T(8,128)S(1)}) %get-tuple-element.1033, (s32[16]{0:T(128)S(1)}, ...), branch_computations={%region_22.23_spmd, %region_23.0_spmd} | conditional | flops 549772288 | bytes 16674920 | solution.py:79
  104.1 3.8 %conditional.12 = ((f32[1,4,512]{2,1,0:T(4,128)S(1)}, f32[1,4,512]{2,1,0:T(4,128)S(1)}, f32[1,4,512,128]{3,2,1,0:T(8,128)S(1)})) conditional(s32[]{:T(128)} %convert_element_type.198, (f32[1,4,512]{2,1,0:T(4,128)S(1)}, f32[1,4,512]{2,1,0:T(4,128)S(1)}, f32[1,4,512,128]{3,2,1,0:T(8,128)S(1)}) %get-tuple-element.1034, (s32[16]{0:T(128)S(1)}, ...), branch_computations={%region_28.29_spmd, %region_29.34_spmd} | conditional | flops 549772288 | bytes 16674920 | solution.py:79
  107.9 3.8 %conditional.13 = ((f32[1,4,512]{2,1,0:T(4,128)S(1)}, f32[1,4,512]{2,1,0:T(4,128)S(1)}, f32[1,4,512,128]{3,2,1,0:T(8,128)S(1)})) conditional(s32[]{:T(128)} %convert_element_type.196, (f32[1,4,512]{2,1,0:T(4,128)S(1)}, f32[1,4,512]{2,1,0:T(4,128)S(1)}, f32[1,4,512,128]{3,2,1,0:T(8,128)S(1)}) %get-tuple-element.1035, (s32[16]{0:T(128)S(1)}, ...), branch_computations={%region_34.35_spmd, %region_35.40_spmd} | conditional | flops 549772288 | bytes 16674920 | solution.py:79
  111.7 4.7 %conditional.14 = ((f32[1,4,512]{2,1,0:T(4,128)S(1)}, f32[1,4,512]{2,1,0:T(4,128)S(1)}, f32[1,4,512,128]{3,2,1,0:T(8,128)S(1)})) conditional(s32[]{:T(128)} %convert_element_type.194, (f32[1,4,512]{2,1,0:T(4,128)S(1)}, f32[1,4,512]{2,1,0:T(4,128)S(1)}, f32[1,4,512,128]{3,2,1,0:T(8,128)S(1)}) %get-tuple-element.1036, (s32[16]{0:T(128)S(1)}, ...), branch_computations={%region_40.41_spmd, %region_41.0_spmd} | conditional | flops 549772288 | bytes 16674920 | solution.py:79
  116.4 4.9 %conditional.15 = ((f32[1,4,512]{2,1,0:T(4,128)S(1)}, f32[1,4,512]{2,1,0:T(4,128)S(1)}, f32[1,4,512,128]{3,2,1,0:T(8,128)S(1)})) conditional(s32[]{:T(128)} %convert_element_type.192, (f32[1,4,512]{2,1,0:T(4,128)S(1)}, f32[1,4,512]{2,1,0:T(4,128)S(1)}, f32[1,4,512,128]{3,2,1,0:T(8,128)S(1)}) %get-tuple-element.1037, (s32[16]{0:T(128)S(1)}, ...), branch_computations={%region_46.47_spmd, %region_47.52_spmd} | conditional | flops 549772288 | bytes 16674920 | solution.py:79
  121.4 4.7 %conditional.16 = ((f32[1,4,512]{2,1,0:T(4,128)S(1)}, f32[1,4,512]{2,1,0:T(4,128)S(1)}, f32[1,4,512,128]{3,2,1,0:T(8,128)S(1)})) conditional(s32[]{:T(128)} %convert_element_type.190, (f32[1,4,512]{2,1,0:T(4,128)S(1)}, f32[1,4,512]{2,1,0:T(4,128)S(1)}, f32[1,4,512,128]{3,2,1,0:T(8,128)S(1)}) %get-tuple-element.1038, (s32[16]{0:T(128)S(1)}, ...), branch_computations={%region_52.53_spmd, %region_53.0_spmd} | conditional | flops 549772288 | bytes 16674920 | solution.py:79
  126.1 3.8 %conditional.17 = ((f32[1,4,512]{2,1,0:T(4,128)S(1)}, f32[1,4,512,128]{3,2,1,0:T(8,128)S(1)})) conditional(s32[]{:T(128)} %convert_element_type.188, (f32[1,4,512]{2,1,0:T(4,128)S(1)}, f32[1,4,512,128]{3,2,1,0:T(8,128)S(1)}) %tuple.93, (s32[16]{0:T(128)S(1)}, s32[]{:T(128)}, s32[]{:T(128)}, bf16[512,1,128]{2,0,1:T(8,128)(2,1)S(1)}, ...), branch_computations={%region_58.59_spmd, %region_59.64_spmd} | conditional | flops 549774336 | bytes 16658528 | solution.py:79
  130.9 14.8 %all_to_all.64 = bf16[8,64,512]{2,1,0:T(8,128)(2,1)S(1)} all-to-all(bf16[8,64,512]{2,1,0:T(8,128)(2,1)S(1)} %convert_element_type.207), channel_id=1, replica_groups=mesh['cp'=64,'hd'=8] {'hd'}, dimensions={0} | all-to-all | bytes 1048576 | tf_op jit(solution)/shard_map/all_to_all | solution.py:121
  (153 shorter events, 64.3 us)
Async XLA Ops:
  0.9 89.7 %copy-start.1 = (s32[16]{0:T(128)S(1)}, s32[16]{0:T(128)}, u32[]{:S(2)}) copy-start(s32[16]{0:T(128)} %param.25) | copy-start | bytes 196
  1.6 10.5 %all-to-all-start = ((bf16[64,8,128]{2,0,1:T(8,128)(2,1)}), bf16[64,8,128]{2,0,1:T(8,128)(2,1)}, u32[]{:S(2)}, u32[]{:S(2)}) async-start(bf16[64,8,128]{2,0,1:T(8,128)(2,1)} %copy_bitcast_fusion.2), calls=%async_computation | async-start | bytes 262144 | tf_op jit(solution)/shard_map/all_to_all | solution.py:87
  12.1 10.1 %all-to-all-start.2 = ((bf16[64,8,128]{2,0,1:T(8,128)(2,1)}), bf16[64,8,128]{2,0,1:T(8,128)(2,1)}, u32[]{:S(2)}, u32[]{:S(2)}) async-start(bf16[64,8,128]{2,0,1:T(8,128)(2,1)} %copy_bitcast_fusion.1), calls=%async_computation.2 | async-start | bytes 262144 | tf_op jit(solution)/shard_map/all_to_all | solution.py:88
  16.1 27.2 %collective-permute-start = (bf16[512,1,128]{2,0,1:T(8,128)(2,1)}, bf16[512,1,128]{2,0,1:T(8,128)(2,1)S(1)}, u32[]{:S(2)}, u32[]{:S(2)}) collective-permute-start(bf16[512,1,128]{2,0,1:T(8,128)(2,1)} %bitcast.127), channel_id=1, source_target_pairs={{0,8},{8,16},{16,24},{24,32},{32,40},{40,48},{48,56},{56,64},{64,7... | collective-permute-start | bytes 393224 | tf_op jit(solution)/shard_map/ppermute | solution.py:17
  22.3 68.2 %all-to-all-start.1 = ((bf16[64,8,512]{2,0,1:T(8,128)(2,1)}), bf16[64,8,512]{2,0,1:T(8,128)(2,1)S(1)}, u32[]{:S(2)}, u32[]{:S(2)}) async-start(bf16[64,8,512]{2,0,1:T(8,128)(2,1)} %bitcast.540), calls=%async_computation.1 | async-start | bytes 1048576 | tf_op jit(solution)/shard_map/all_to_all | solution.py:86
  26.2 22.1 %collective-permute-start.1 = (bf16[512,1,128]{2,0,1:T(8,128)(2,1)}, bf16[512,1,128]{2,0,1:T(8,128)(2,1)S(1)}, u32[]{:S(2)}, u32[]{:S(2)}) collective-permute-start(bf16[512,1,128]{2,0,1:T(8,128)(2,1)} %bitcast.130), channel_id=1, source_target_pairs={{0,8},{8,16},{16,24},{24,32},{32,40},{40,48},{48,56},{56,64},{64,7... | collective-permute-start | bytes 393224 | tf_op jit(solution)/shard_map/ppermute | solution.py:17
  29.7 22.1 %collective-permute-start.2 = (bf16[512,1,128]{2,0,1:T(8,128)(2,1)}, bf16[512,1,128]{2,0,1:T(8,128)(2,1)S(1)}, u32[]{:S(2)}, u32[]{:S(2)}) collective-permute-start(bf16[512,1,128]{2,0,1:T(8,128)(2,1)} %bitcast.127), channel_id=1, source_target_pairs={{0,16},{8,24},{16,32},{24,40},{32,48},{40,56},{48,64},{56,72},{64,... | collective-permute-start | bytes 393224 | tf_op jit(solution)/shard_map/ppermute | solution.py:17
  34.5 20.2 %collective-permute-start.3 = (bf16[512,1,128]{2,0,1:T(8,128)(2,1)}, bf16[512,1,128]{2,0,1:T(8,128)(2,1)S(1)}, u32[]{:S(2)}, u32[]{:S(2)}) collective-permute-start(bf16[512,1,128]{2,0,1:T(8,128)(2,1)} %bitcast.130), channel_id=1, source_target_pairs={{0,16},{8,24},{16,32},{24,40},{32,48},{40,56},{48,64},{56,72},{64,... | collective-permute-start | bytes 393224 | tf_op jit(solution)/shard_map/ppermute | solution.py:17
  38.4 19.8 %collective-permute-start.4 = (bf16[512,1,128]{2,0,1:T(8,128)(2,1)}, bf16[512,1,128]{2,0,1:T(8,128)(2,1)S(1)}, u32[]{:S(2)}, u32[]{:S(2)}) collective-permute-start(bf16[512,1,128]{2,0,1:T(8,128)(2,1)} %bitcast.127), channel_id=1, source_target_pairs={{0,24},{8,32},{16,40},{24,48},{32,56},{40,64},{48,72},{56,80},{64,... | collective-permute-start | bytes 393224 | tf_op jit(solution)/shard_map/ppermute | solution.py:17
  43.3 17.6 %collective-permute-start.5 = (bf16[512,1,128]{2,0,1:T(8,128)(2,1)}, bf16[512,1,128]{2,0,1:T(8,128)(2,1)S(1)}, u32[]{:S(2)}, u32[]{:S(2)}) collective-permute-start(bf16[512,1,128]{2,0,1:T(8,128)(2,1)} %bitcast.130), channel_id=1, source_target_pairs={{0,24},{8,32},{16,40},{24,48},{32,56},{40,64},{48,72},{56,80},{64,... | collective-permute-start | bytes 393224 | tf_op jit(solution)/shard_map/ppermute | solution.py:17
  48.3 18.7 %collective-permute-start.6 = (bf16[512,1,128]{2,0,1:T(8,128)(2,1)}, bf16[512,1,128]{2,0,1:T(8,128)(2,1)S(1)}, u32[]{:S(2)}, u32[]{:S(2)}) collective-permute-start(bf16[512,1,128]{2,0,1:T(8,128)(2,1)} %bitcast.127), channel_id=1, source_target_pairs={{0,32},{8,40},{16,48},{24,56},{32,64},{40,72},{48,80},{56,88},{64,... | collective-permute-start | bytes 393224 | tf_op jit(solution)/shard_map/ppermute | solution.py:17
  51.7 17.9 %collective-permute-start.7 = (bf16[512,1,128]{2,0,1:T(8,128)(2,1)}, bf16[512,1,128]{2,0,1:T(8,128)(2,1)S(1)}, u32[]{:S(2)}, u32[]{:S(2)}) collective-permute-start(bf16[512,1,128]{2,0,1:T(8,128)(2,1)} %bitcast.130), channel_id=1, source_target_pairs={{0,32},{8,40},{16,48},{24,56},{32,64},{40,72},{48,80},{56,88},{64,... | collective-permute-start | bytes 393224 | tf_op jit(solution)/shard_map/ppermute | solution.py:17
  54.7 6.2 %copy-start.6 = (bf16[512,1,128]{2,0,1:T(8,128)(2,1)}, bf16[512,1,128]{2,0,1:T(8,128)(2,1)S(1)}, u32[]{:S(2)}) copy-start(bf16[512,1,128]{2,0,1:T(8,128)(2,1)S(1)} %collective-permute-done.3) | copy-start | bytes 393220
  54.7 19.2 %collective-permute-start.8 = (bf16[512,1,128]{2,0,1:T(8,128)(2,1)}, bf16[512,1,128]{2,0,1:T(8,128)(2,1)S(1)}, u32[]{:S(2)}, u32[]{:S(2)}) collective-permute-start(bf16[512,1,128]{2,0,1:T(8,128)(2,1)} %bitcast.127), channel_id=1, source_target_pairs={{0,40},{8,48},{16,56},{24,64},{32,72},{40,80},{48,88},{56,96},{64,... | collective-permute-start | bytes 393224 | tf_op jit(solution)/shard_map/ppermute | solution.py:17
  58.1 19.4 %collective-permute-start.9 = (bf16[512,1,128]{2,0,1:T(8,128)(2,1)}, bf16[512,1,128]{2,0,1:T(8,128)(2,1)}, u32[]{:S(2)}, u32[]{:S(2)}) collective-permute-start(bf16[512,1,128]{2,0,1:T(8,128)(2,1)} %bitcast.130), channel_id=1, source_target_pairs={{0,40},{8,48},{16,56},{24,64},{32,72},{40,80},{48,88},{56,96},{64,... | collective-permute-start | bytes 393224 | tf_op jit(solution)/shard_map/ppermute | solution.py:17
  60.9 8.8 %copy-start.4 = (bf16[512,1,128]{2,0,1:T(8,128)(2,1)}, bf16[512,1,128]{2,0,1:T(8,128)(2,1)S(1)}, u32[]{:S(2)}) copy-start(bf16[512,1,128]{2,0,1:T(8,128)(2,1)S(1)} %collective-permute-done.5) | copy-start | bytes 393220
  60.9 19.7 %collective-permute-start.10 = (bf16[512,1,128]{2,0,1:T(8,128)(2,1)}, bf16[512,1,128]{2,0,1:T(8,128)(2,1)S(1)}, u32[]{:S(2)}, u32[]{:S(2)}) collective-permute-start(bf16[512,1,128]{2,0,1:T(8,128)(2,1)} %bitcast.127), channel_id=1, source_target_pairs={{0,48},{8,56},{16,64},{24,72},{32,80},{40,88},{48,96},{56,104},{64... | collective-permute-start | bytes 393224 | tf_op jit(solution)/shard_map/ppermute | solution.py:17
  67.0 49.4 %collective-permute-start.11 = (bf16[512,1,128]{2,0,1:T(8,128)(2,1)}, bf16[512,1,128]{2,0,1:T(8,128)(2,1)}, u32[]{:S(2)}, u32[]{:S(2)}) collective-permute-start(bf16[512,1,128]{2,0,1:T(8,128)(2,1)} %bitcast.130), channel_id=1, source_target_pairs={{0,48},{8,56},{16,64},{24,72},{32,80},{40,88},{48,96},{56,104},{64... | collective-permute-start | bytes 393224 | tf_op jit(solution)/shard_map/ppermute | solution.py:17
  69.7 6.1 %copy-start.2 = (bf16[512,1,128]{2,0,1:T(8,128)(2,1)}, bf16[512,1,128]{2,0,1:T(8,128)(2,1)S(1)}, u32[]{:S(2)}) copy-start(bf16[512,1,128]{2,0,1:T(8,128)(2,1)S(1)} %collective-permute-done.7) | copy-start | bytes 393220
  69.7 51.7 %collective-permute-start.12 = (bf16[512,1,128]{2,0,1:T(8,128)(2,1)}, bf16[512,1,128]{2,0,1:T(8,128)(2,1)S(1)}, u32[]{:S(2)}, u32[]{:S(2)}) collective-permute-start(bf16[512,1,128]{2,0,1:T(8,128)(2,1)} %bitcast.127), channel_id=1, source_target_pairs={{0,56},{8,64},{16,72},{24,80},{32,88},{40,96},{48,104},{56,112},{6... | collective-permute-start | bytes 393224 | tf_op jit(solution)/shard_map/ppermute | solution.py:17
  73.9 47.5 %collective-permute-start.13 = (bf16[512,1,128]{2,0,1:T(8,128)(2,1)}, bf16[512,1,128]{2,0,1:T(8,128)(2,1)}, u32[]{:S(2)}, u32[]{:S(2)}) collective-permute-start(bf16[512,1,128]{2,0,1:T(8,128)(2,1)} %bitcast.130), channel_id=1, source_target_pairs={{0,56},{8,64},{16,72},{24,80},{32,88},{40,96},{48,104},{56,112},{6... | collective-permute-start | bytes 393224 | tf_op jit(solution)/shard_map/ppermute | solution.py:17
  77.5 48.6 %collective-permute-start.14 = (bf16[512,1,128]{2,0,1:T(8,128)(2,1)}, bf16[512,1,128]{2,0,1:T(8,128)(2,1)S(1)}, u32[]{:S(2)}, u32[]{:S(2)}) collective-permute-start(bf16[512,1,128]{2,0,1:T(8,128)(2,1)} %bitcast.127), channel_id=1, source_target_pairs={{0,64},{8,72},{16,80},{24,88},{32,96},{40,104},{48,112},{56,120},{... | collective-permute-start | bytes 393224 | tf_op jit(solution)/shard_map/ppermute | solution.py:17
  80.6 45.5 %collective-permute-start.15 = (bf16[512,1,128]{2,0,1:T(8,128)(2,1)}, bf16[512,1,128]{2,0,1:T(8,128)(2,1)S(1)}, u32[]{:S(2)}, u32[]{:S(2)}) collective-permute-start(bf16[512,1,128]{2,0,1:T(8,128)(2,1)} %bitcast.130), channel_id=1, source_target_pairs={{0,64},{8,72},{16,80},{24,88},{32,96},{40,104},{48,112},{56,120},{... | collective-permute-start | bytes 393224 | tf_op jit(solution)/shard_map/ppermute | solution.py:17
  90.6 5.6 %copy-start.9 = (bf16[512,1,128]{2,0,1:T(8,128)(2,1)S(1)}, bf16[512,1,128]{2,0,1:T(8,128)(2,1)}, u32[]{:S(2)}) copy-start(bf16[512,1,128]{2,0,1:T(8,128)(2,1)} %copy-done.8) | copy-start | bytes 393220
  (5 other events, 16.0 us)
where the time goes:
time: 148 us; the launch traced here: 147 us
  starting transfers between devices  68.9 us (47%)
  matrix products  26.1 us (18%)
  blocking collectives  14.8 us (10%)
  other arithmetic  13.8 us (9%)
  waiting for transfers between devices  8.31 us (6%)
  between operations  6.89 us (5%)
  local copies, waits for them, and re-layouts  6.75 us (5%)
    ppermute x16, starting transfers between devices, from_behind(): return lax.ppermute(block, axis, route)  56.7 us
    dot_general x9, matrix products, attend(): jnp.einsum('hgqk,khd->hgqd', weights.astype(jnp.bfloat16), values_part, p...  17.1 us
    all_to_all x1, blocking collectives, per_device(): return lax.all_to_all(result, 'hd', split_axis=0, concat_axis=1, tiled=True)  14.8 us
    dot_general x9, matrix products, attend(): jnp.einsum('qhgd,khd->hgqk', query, keys_part, preferred_element_type=jnp...  8.98 us
    reduce_sum x9, other arithmetic, attend(): new_total = old_total * rescale + jnp.sum(weights, axis=3)  8.25 us
    all_to_all x1, waiting for transfers between devices, per_device(): lax.all_to_all(keys, 'hd', split_axis=1, concat_axis=0, tiled=True)  4.65 us
    all_to_all x1, starting transfers between devices, per_device(): lax.all_to_all(keys, 'hd', split_axis=1, concat_axis=0, tiled=True)  4.3 us
    all_to_all x1, starting transfers between devices, per_device(): lax.all_to_all(values, 'hd', split_axis=1, concat_axis=0, tiled=True)  3.99 us
  transfers between devices with their start and end apart: 19, of which 4 were waited for; matrix products, arithmetic and copies ran while one was open for 27% of the time, Pallas kernels for 0%

commit v1 on v0

v1 whole, which is shorter than its diff:
```python
import functools
import math

import jax
import jax.numpy as jnp
from jax import lax
from jax.experimental import pallas as pl
from jax.experimental.pallas import tpu as pltpu
from jax.sharding import Mesh, PartitionSpec as P

D_HEAD = 128
BLOCK = 512
MAX_DOC = 4096
PLANE = 32
ROW = 8
SUPER = 2 * BLOCK
SLOTS = (MAX_DOC + SUPER) // BLOCK
FLOOR = -1.0e30
SCALE = D_HEAD**-0.5 * math.log2(math.e)
PART = 128
ROWS = 2 * BLOCK


def attend(late, starts, q_ref, *refs):
    if late:
        z2, yb, yac, xb, xc, acc_in, top_in, out_ref = refs[:8]
    else:
        own, z1, xa, acc_out, top_out = refs[:5]
    (k_ref, v_ref, qx_ref, scores_a, scores_b, weights, acc, top_ref, shift,
     k_sem, v_sem) = refs[-11:]
    me = lax.axis_index("d")
    z = me // PLANE
    pair = lax.rem(me // (2 * ROW), 2)
    core = lax.rem(me, 2)
    s_first = (z * 2 + pair) * SUPER

    firsts, lasts, counts = [], [], []
    for pos in range(2):
        q_start = s_first + pos * BLOCK
        first = jnp.int32(0)
        last = jnp.int32(0)
        for i in range(starts.shape[0]):
            s = starts[i]
            first = jnp.where(s <= q_start, s, first)
            last = jnp.where(s <= q_start + BLOCK - 1, s, last)
        firsts.append(first)
        lasts.append(last)
        counts.append((q_start - first + BLOCK - 1) // BLOCK)
    lowest = jnp.minimum(SLOTS - 2 - counts[0], SLOTS - 1 - counts[1])

    def fetch(j, mine, mine_row, other, other_row, when):
        swapped = lax.rem(pair + j, 2)
        for half in range(2):
            slot = SLOTS - 2 - 2 * j + lax.bitwise_xor(half, swapped)
            to = pl.ds(pl.multiple_of(slot * BLOCK, BLOCK), BLOCK)
            for c in range(2):
                @pl.when((core == c) & (slot >= lowest) & when)
                def _():
                    mine_at = mine.at[pl.ds(mine_row + half * BLOCK, BLOCK)]
                    other_at = other.at[pl.ds(other_row + half * BLOCK, BLOCK)]
                    k_src, v_src = (mine_at, other_at) if c == 0 else (other_at, mine_at)
                    pltpu.make_async_copy(k_src, k_ref.at[to, 0:D_HEAD], k_sem.at[slot]).start()
                    pltpu.make_async_copy(v_src, v_ref.at[to, 0:D_HEAD], v_sem.at[slot]).start()

    always = me >= 0
    if late:
        fetch(1, yac, 0, xc, 0, pair == 1)
        fetch(1, yb, 0, xb, SUPER, pair == 0)
        fetch(3, yb, 0, xb, SUPER, pair == 1)
        fetch(3, yac, 0, xc, 0, pair == 0)
        fetch(4, z2, 0, xb, 0, always)
        ranges = ((0, 4), (6, 8))
        any_block = z2
    else:
        fetch(0, own, 0, xa, 0, always)
        fetch(2, z1, 0, xa, SUPER, always)
        ranges = ((4, 6), (8, 10))
        any_block = own

    lane = lax.broadcasted_iota(jnp.int32, (BLOCK, D_HEAD), 1)
    row = lax.broadcasted_iota(jnp.int32, (BLOCK, D_HEAD), 0)
    limits = jnp.where(lane == 0, firsts[0], jnp.where(lane == 1, firsts[1],
                       jnp.where(lane == 2, lasts[0], jnp.where(lane == 3, lasts[1], 0))))
    base = s_first - (SLOTS - 2) * BLOCK
    behind = limits - row - base

    def bias(slot, carry):
        to = pl.ds(pl.multiple_of(slot * BLOCK, BLOCK), BLOCK)
        ahead = behind > slot * BLOCK
        k_ref[to, D_HEAD:] = jnp.where(ahead, FLOOR, 0.0).astype(jnp.bfloat16)
        v_ref[to, D_HEAD:] = jnp.ones((BLOCK, D_HEAD), jnp.bfloat16)
        return carry

    def arrive(slot, carry):
        to = pl.ds(pl.multiple_of(slot * BLOCK, BLOCK), BLOCK)
        rows = pl.ds(0, BLOCK)
        pltpu.make_async_copy(any_block.at[rows], k_ref.at[to, 0:D_HEAD], k_sem.at[slot]).wait()
        pltpu.make_async_copy(any_block.at[rows], v_ref.at[to, 0:D_HEAD], v_sem.at[slot]).wait()
        return carry

    for low, high in ranges:
        lax.fori_loop(jnp.maximum(lowest, low), high, bias, 0)

    groups = [slice(g, g + D_HEAD) for g in range(0, BLOCK, D_HEAD)]
    parts = [slice(r, r + PART) for r in range(0, ROWS, PART)]

    class Tile:
        def __init__(self, half):
            self.half = half
            self.scores = scores_b if half else scores_a
            pos = lax.bitwise_xor(half, pair)
            self.own = SLOTS - 2 + pos
            n = jnp.where(pos == 0, counts[0], counts[1])
            border = jnp.where(pos == 0, lasts[0], lasts[1]) - s_first - pos * BLOCK
            column = jnp.where(row >= border, pos + 2, pos)
            marks = jnp.where((lane == pos) | (lane == column), 1.0, 0.0).astype(jnp.bfloat16)
            for head in range(2):
                to = slice(head * BLOCK, (head + 1) * BLOCK)
                at = slice(head * D_HEAD, (head + 1) * D_HEAD)
                qx_ref[half, to, 0:D_HEAD] = q_ref[half * BLOCK:(half + 1) * BLOCK, at]
                qx_ref[half, to, D_HEAD:] = marks
            m = n - pos
            if late:
                self.steps = jnp.clip(m, 0, 2) + jnp.clip(m - 4, 0, 4)
                self.distance = lambda i: jnp.where(i < 2, i + 1, i + 3) + pos
            else:
                beside = jnp.where((pos == 1) & (n >= 1), 1, 0)
                self.steps = beside + jnp.clip(m - 2, 0, 2)
                self.distance = lambda i: jnp.where((pos == 1) & (i == 0), 1, i + 3)

        def keys(self, d):
            return pl.ds(pl.multiple_of((self.own - d) * BLOCK, BLOCK), BLOCK)

        def weigh(self, b, d):
            for r in parts:
                for g in groups:
                    p = jnp.exp2(self.scores[b, r, g] * SCALE - shift[r, :])
                    weights[r, g] = p.astype(jnp.bfloat16)
            return jnp.dot(weights[...], v_ref[self.keys(d), :], preferred_element_type=jnp.float32)

        def fresh(self, b, d):
            self.scores[b] = lax.dot_general(
                qx_ref[self.half], k_ref[self.keys(d), :], (((1,), (1,)), ((), ())),
                preferred_element_type=jnp.float32)
            for r in parts:
                top = top_ref[r, :]
                query = slice(r.start % BLOCK, r.start % BLOCK + PART)
                for g in groups:
                    part = self.scores[b, r, g]
                    if isinstance(d, int):
                        part = jnp.where(lane[query] + g.start <= row[query], part, FLOOR)
                        self.scores[b, r, g] = part
                    top = jnp.maximum(top, part)
                top_ref[r, :] = top

    def loop(first, stop, old, young):
        def go(i, carry):
            b = i if late else i + 1
            if old:
                acc[...] += old.weigh(b, old.distance(i))
            if young:
                young.fresh(b, young.distance(i))
            return carry

        lax.fori_loop(first, stop, go, 0)

    tiles = [Tile(half) for half in range(2)]
    for low, high in ranges:
        lax.fori_loop(jnp.maximum(lowest, low), high, arrive, 0)
    for t in range(3):
        cur = tiles[t - 1] if t > 0 else None
        new = tiles[t] if t < 2 else None
        if cur and not late:
            acc[...] = cur.weigh(0, 0)
        if new and late:
            top_ref[...] = top_in[new.half]
        elif new:
            top_ref[...] = jnp.full((ROWS, D_HEAD), FLOOR, jnp.float32)
            new.fresh(0, 0)
        if cur and new:
            both = jnp.minimum(cur.steps, new.steps)
            loop(0, both, cur, new)
            loop(both, cur.steps, cur, None)
            loop(both, new.steps, None, new)
        elif cur:
            loop(0, cur.steps, cur, None)
        else:
            loop(0, new.steps, None, new)
        if cur and late:
            for head in range(2):
                r = slice(head * BLOCK, (head + 1) * BLOCK)
                mixed = acc[r, 0:D_HEAD] / acc[r, D_HEAD:]
                out_ref[cur.half * BLOCK:(cur.half + 1) * BLOCK,
                        head * D_HEAD:(head + 1) * D_HEAD] = mixed.astype(jnp.bfloat16)
        elif cur:
            acc_out[cur.half] = acc[...]
        if new:
            for r in parts:
                top = jnp.max(top_ref[r, :], axis=1, keepdims=True)
                top = jnp.broadcast_to(top, (PART, D_HEAD))
                shift[r, :] = top * SCALE
                if late:
                    rescale = jnp.exp2((top_in[new.half, r, :] - top) * SCALE)
                    acc[r, 0:D_HEAD] = acc_in[new.half, r, 0:D_HEAD] * rescale
                    acc[r, D_HEAD:] = acc_in[new.half, r, D_HEAD:] * rescale
                else:
                    top_out[new.half, r, :] = top


def attention(late, doc_starts, q, blocks, state=()):
    vmem = pl.BlockSpec(memory_space=pltpu.VMEM)
    if late:
        out_shape, out_specs = jax.ShapeDtypeStruct(q.shape, jnp.bfloat16), vmem
    else:
        out_shape = (jax.ShapeDtypeStruct((2, ROWS, 2 * D_HEAD), jnp.float32),
                     jax.ShapeDtypeStruct((2, ROWS, D_HEAD), jnp.float32))
        out_specs = (vmem,) * 2
    scores = pltpu.VMEM((6 if late else 4, ROWS, BLOCK), jnp.float32)
    return pl.pallas_call(
        functools.partial(attend, late),
        out_shape=out_shape,
        in_specs=[pl.BlockSpec(memory_space=pltpu.SMEM), vmem]
        + [pl.BlockSpec(memory_space=pl.ANY)] * len(blocks) + [vmem] * len(state),
        out_specs=out_specs,
        scratch_shapes=[
            pltpu.VMEM((SLOTS * BLOCK, 2 * D_HEAD), jnp.bfloat16),
            pltpu.VMEM((SLOTS * BLOCK, 2 * D_HEAD), jnp.bfloat16),
            pltpu.VMEM((2, ROWS, 2 * D_HEAD), jnp.bfloat16),
            scores,
            scores,
            pltpu.VMEM((ROWS, BLOCK), jnp.bfloat16),
            pltpu.VMEM((ROWS, 2 * D_HEAD), jnp.float32),
            pltpu.VMEM((ROWS, D_HEAD), jnp.float32),
            pltpu.VMEM((ROWS, D_HEAD), jnp.float32),
            pltpu.SemaphoreType.DMA((SLOTS,)),
            pltpu.SemaphoreType.DMA((SLOTS,)),
        ],
        compiler_params=pltpu.CompilerParams(vmem_limit_bytes=44 * 1024 * 1024),
        cost_estimate=pl.CostEstimate(
            flops=(3 if late else 2) * 10**9, bytes_accessed=4 * 10**6, transcendentals=3 * 10**6
        ),
        name="late_blocks" if late else "early_blocks",
    )(doc_starts, q, *blocks, *state)


def per_device(queries, keys, values, doc_starts):
    devices = lax.axis_size("d")
    rows = queries.shape[0]
    groups = []
    for z in range(0, devices, PLANE):
        groups.append(list(range(z, z + 16)))
        groups.append(list(range(z + 24, z + 32)) + list(range(z + 16, z + 24)))

    def exchange(x):
        return lax.all_to_all(
            x, "d", split_axis=0, concat_axis=0, axis_index_groups=groups, tiled=True
        )

    def move(x, rule):
        pairs = []
        for d in range(devices):
            z, y = d // PLANE, d // ROW % 4
            to = rule(d, z, y)
            if to is not None and to < devices:
                pairs.append((d, to))
        return lax.ppermute(x, "d", pairs)

    def mirror(d, y):
        return d + ROW * (3 - 2 * y)

    def cores(x):
        return move(x, lambda d, z, y: d ^ 1)

    heads = keys.shape[1] // D_HEAD
    kv = jnp.stack(
        [keys.reshape(rows, heads, D_HEAD), values.reshape(rows, heads, D_HEAD)], axis=2
    ).reshape(rows, 2 * heads, D_HEAD).transpose(1, 0, 2)
    own = exchange(kv).reshape(SUPER, D_HEAD)
    q = queries.reshape(rows, 2 * heads, 2 * D_HEAD).transpose(1, 0, 2)
    q = exchange(q).reshape(SUPER, 2 * D_HEAD)

    first_pair = (lax.axis_index("d") & (2 * ROW)) == 0
    z1 = move(own, lambda d, z, y: d + PLANE)
    z2 = move(z1, lambda d, z, y: d + PLANE if z > 0 else None)
    yb = move(z1, lambda d, z, y: mirror(d, y))
    xa = cores(jnp.concatenate([own, z1]))
    z2, q = lax.optimization_barrier((z2, q))
    yac = move(jnp.where(first_pair, own, z2), lambda d, z, y: mirror(d, y))
    xb = cores(jnp.concatenate([z2, yb]))
    state = attention(False, doc_starts, q, (own, z1, xa))
    yac, state = lax.optimization_barrier((yac, state))
    xc = cores(yac)
    out = attention(True, doc_starts, q, (z2, yb, yac, xb, xc), state)
    out = exchange(out.reshape(2 * heads, rows, 2 * D_HEAD))
    return out.transpose(1, 0, 2).reshape(rows, heads * 4 * D_HEAD)


def solution(mesh):
    mesh = Mesh(mesh.devices.reshape(-1), ("d",))
    rows = P("d", None)
    return jax.shard_map(
        per_device, mesh=mesh, in_specs=(rows, rows, rows, P()), out_specs=rows, check_vma=False
    )
```

time: 148 us -> 80.7 us (0.55)
  the two profiles are of different devices: /device:TPU:160 before, /device:TPU:209 now
where the time goes in v1:
time: 80.7 us; the launch traced here: 80.2 us
  blocking collectives  27.2 us (34%)
  starting transfers between devices  27 us (33%)
  Pallas kernels  19.5 us (24%)
  local copies, waits for them, and re-layouts  3.63 us (4%)
  waiting for transfers between devices  2.67 us (3%)
    all_to_all x2, blocking collectives, exchange(): lax.all_to_all(x, 'd', split_axis=0, concat_axis=0, axis_index_groups=gro...  27.2 us
    ppermute x7, starting transfers between devices, move(): return lax.ppermute(x, 'd', pairs)  21.6 us
    pallas_call x2, Pallas kernels, attention(): pl.pallas_call(functools.partial(attend, late), out_shape=out_shape, in_s...  19.5 us
    all_to_all x1, starting transfers between devices, exchange(): lax.all_to_all(x, 'd', split_axis=0, concat_axis=0, axis_index_groups=gro...  5.32 us
    ppermute x7, waiting for transfers between devices, move(): return lax.ppermute(x, 'd', pairs)  2.67 us
    unnamed x6, local copies, waits for them, and re-layouts  1.92 us
  transfers between devices with their start and end apart: 8, of which 3 were waited for; matrix products, arithmetic and copies ran while one was open for 1% of the time, Pallas kernels for 10%

profile of v1, /device:TPU:209, one launch (start us, length us, event | category | flops | bytes accessed | tf_op | source)
XLA Modules:
  0.0 80.2 jit_solution(11415227591387076787)
XLA Ops:
  0.0 1.0 %copy.11 = bf16[8,8,8,128]{3,2,1,0:T(8,128)(2,1)S(1)} copy(bf16[8,8,8,128]{3,1,2,0:T(8,128)(2,1)} %bitcast.36) | data formatting | bytes 262144
  1.0 0.9 %copy.10 = bf16[8,8,8,128]{3,2,1,0:T(8,128)(2,1)S(1)} copy(bf16[8,8,8,128]{3,1,2,0:T(8,128)(2,1)} %bitcast.37) | data formatting | bytes 262144
  2.0 12.4 %all_to_all.15 = bf16[16,64,128]{2,1,0:T(8,128)(2,1)S(1)} all-to-all(bf16[16,64,128]{2,1,0:T(8,128)(2,1)S(1)} %bitcast.32), channel_id=1, replica_groups={{0,1,2,3,4,5,6,7,8,9,10,11,12,13,14,15},{24,25,26,27,28,29,30,31,16,17,..., dimensions={0} | all-to-all | bytes 524288 | tf_op jit(solution)/shard_map/all_to_all | solution.py:255
  14.4 3.5 %collective-permute-start = (bf16[1024,128]{1,0:T(8,128)(2,1)S(1)}, bf16[1024,128]{1,0:T(8,128)(2,1)S(1)}, u32[]{:S(2)}, u32[]{:S(2)}) collective-permute-start(bf16[1024,128]{1,0:T(8,128)(2,1)S(1)} %bitcast.25), channel_id=1, source_target_pairs={{0,32},{1,33},{2,34},{3,35},{4,36},{5,37},{6,38},{7,39},{8,40},{9,... | collective-permute-start | bytes 786440 | tf_op jit(solution)/shard_map/ppermute | solution.py:266
  17.9 0.8 %copy.13 = bf16[8,16,8,256]{3,2,0,1:T(8,128)(2,1)} copy(bf16[8,16,8,256]{3,2,1,0:T(8,128)(2,1)S(1)} %bitcast.33) | data formatting | bytes 1048576 | tf_op jit(solution)/shard_map/reshape | solution.py:279
  18.8 5.3 %all-to-all-start.1 = ((bf16[16,64,256]{2,1,0:T(8,128)(2,1)}), bf16[16,64,256]{2,1,0:T(8,128)(2,1)S(1)}, u32[]{:S(2)}, u32[]{:S(2)}) async-start(bf16[16,64,256]{2,1,0:T(8,128)(2,1)} %bitcast.24), calls=%async_computation.1 | async-start | bytes 1048576 | tf_op jit(solution)/shard_map/all_to_all | solution.py:255
  24.1 0.0 collective-permute-done.refs_1_
  24.1 4.8 %collective-permute-start.1 = (bf16[1024,128]{1,0:T(8,128)(2,1)S(1)}, bf16[1024,128]{1,0:T(8,128)(2,1)S(1)}, u32[]{:S(2)}, u32[]{:S(2)}) collective-permute-start(bf16[1024,128]{1,0:T(8,128)(2,1)S(1)} %collective-permute-done.refs_1_), channel_id=1, source_target_pairs={{32,64},{33,65},{34,66},{35,67},{36,68},{37,69},{38,70},{39,71},{4... | collective-permute-start | bytes 786440 | tf_op jit(solution)/shard_map/ppermute | solution.py:266
  28.9 2.1 %collective-permute-start.2 = (bf16[1024,128]{1,0:T(8,128)(2,1)S(1)}, bf16[1024,128]{1,0:T(8,128)(2,1)S(1)}, u32[]{:S(2)}, u32[]{:S(2)}) collective-permute-start(bf16[1024,128]{1,0:T(8,128)(2,1)S(1)} %collective-permute-done.refs_1_), channel_id=1, source_target_pairs={{0,24},{1,25},{2,26},{3,27},{4,28},{5,29},{6,30},{7,31},{8,16},{9,... | collective-permute-start | bytes 786440 | tf_op jit(solution)/shard_map/ppermute | solution.py:266
  31.0 2.8 %collective-permute-start.4 = (bf16[2048,128]{1,0:T(8,128)(2,1)S(1)}, bf16[2048,128]{1,0:T(8,128)(2,1)S(1)}, u32[]{:S(2)}, u32[]{:S(2)}) collective-permute-start(bf16[2048,128]{1,0:T(8,128)(2,1)S(1)} %pad_maximum_fusion), channel_id=1, source_target_pairs={{0,1},{1,0},{2,3},{3,2},{4,5},{5,4},{6,7},{7,6},{8,9},{9,8},{10,11... | collective-permute-start | bytes 1572872 | tf_op jit(solution)/shard_map/ppermute | solution.py:266
  33.8 0.0 all-to-all-done.1
  33.8 0.3 collective-permute-done.1.refs_0_
  34.2 2.9 %collective-permute-start.3 = (bf16[1024,128]{1,0:T(8,128)(2,1)S(1)}, bf16[1024,128]{1,0:T(8,128)(2,1)S(1)}, u32[]{:S(2)}, u32[]{:S(2)}) collective-permute-start(bf16[1024,128]{1,0:T(8,128)(2,1)S(1)} %broadcast_select_fusion), channel_id=1, source_target_pairs={{0,24},{1,25},{2,26},{3,27},{4,28},{5,29},{6,30},{7,31},{8,16},{9,... | collective-permute-start | bytes 786440 | tf_op jit(solution)/shard_map/ppermute | solution.py:266
  37.1 0.8 %collective-permute-done.2.refs_1_ = bf16[1024,128]{1,0:T(8,128)(2,1)S(1)} collective-permute-done((bf16[1024,128]{1,0:T(8,128)(2,1)S(1)}, bf16[1024,128]{1,0:T(8,128)(2,1)S(1)}, u32[]{:S(2)}, u32[]{:S(2)}) %collective-permute-start.2) | collective-permute-done | bytes 262176 | tf_op jit(solution)/shard_map/ppermute | solution.py:266
  38.0 3.6 %collective-permute-start.5 = (bf16[2048,128]{1,0:T(8,128)(2,1)S(1)}, bf16[2048,128]{1,0:T(8,128)(2,1)S(1)}, u32[]{:S(2)}, u32[]{:S(2)}) collective-permute-start(bf16[2048,128]{1,0:T(8,128)(2,1)S(1)} %pad_maximum_fusion.1), channel_id=1, source_target_pairs={{0,1},{1,0},{2,3},{3,2},{4,5},{5,4},{6,7},{7,6},{8,9},{9,8},{10,11... | collective-permute-start | bytes 1572872 | tf_op jit(solution)/shard_map/ppermute | solution.py:266
  41.6 0.0 collective-permute-done.4.refs_2_
  41.7 8.3 %early_blocks.1 = (f32[2,1024,256]{2,1,0:T(8,128)S(1)}, f32[2,1024,128]{2,1,0:T(8,128)S(1)}) custom-call(s32[16]{0:T(128)S(1)} %copy-done, bf16[1024,256]{1,0:T(8,128)(2,1)S(1)} %bitcast.28, bf16[1024,128]{1,0:T(8,128)(2,1)S(1)} %bitcast.27, bf16[1024,128]{1,0:T(8,128)(2,1)S(1)} %collective-permute-done.refs_1_, ...), custom_call_target="tpu_custom_call" | custom-call | flops 2000000000 | bytes 4000000 | tf_op jit(solution)/shard_map/early_blocks/pallas_call | solution.py:219
  49.9 0.0 collective-permute-done.3.refs_2_
  50.0 1.9 %collective-permute-start.6 = (bf16[1024,128]{1,0:T(8,128)(2,1)S(1)}, bf16[1024,128]{1,0:T(8,128)(2,1)S(1)}, u32[]{:S(2)}, u32[]{:S(2)}) collective-permute-start(bf16[1024,128]{1,0:T(8,128)(2,1)S(1)} %collective-permute-done.3.refs_2_), channel_id=1, source_target_pairs={{0,1},{1,0},{2,3},{3,2},{4,5},{5,4},{6,7},{7,6},{8,9},{9,8},{10,11... | collective-permute-start | bytes 786440 | tf_op jit(solution)/shard_map/ppermute | solution.py:266
  51.9 0.0 collective-permute-done.5.refs_3_
  51.9 1.5 %collective-permute-done.6.refs_4_ = bf16[1024,128]{1,0:T(8,128)(2,1)S(1)} collective-permute-done((bf16[1024,128]{1,0:T(8,128)(2,1)S(1)}, bf16[1024,128]{1,0:T(8,128)(2,1)S(1)}, u32[]{:S(2)}, u32[]{:S(2)}) %collective-permute-start.6) | collective-permute-done | bytes 262176 | tf_op jit(solution)/shard_map/ppermute | solution.py:266
  53.4 11.2 %late_blocks.1 = bf16[1024,256]{1,0:T(8,128)(2,1)S(1)} custom-call(s32[16]{0:T(128)S(1)} %copy-done, bf16[1024,256]{1,0:T(8,128)(2,1)S(1)} %bitcast.29, bf16[1024,128]{1,0:T(8,128)(2,1)S(1)} %collective-permute-done.1.refs_0_, bf16[1024,128]{1,0:T(8,128)(2,1)S(1)} %collective-permute-done.2.refs_1_, bf16[1024,128]{1,0:T(8,128)(2,1)S(1)} %collective-permute-done.3.refs_2_, ...), custom_call_target="tpu_custom_call" | custom-call | flops 3000000000 | bytes 4000000 | tf_op jit(solution)/shard_map/late_blocks/pallas_call | solution.py:219
  64.6 14.8 %all_to_all.16 = bf16[16,64,256]{2,1,0:T(8,128)(2,1)S(1)} all-to-all(bf16[16,64,256]{2,1,0:T(8,128)(2,1)S(1)} %bitcast.30), channel_id=1, replica_groups={{0,1,2,3,4,5,6,7,8,9,10,11,12,13,14,15},{24,25,26,27,28,29,30,31,16,17,..., dimensions={0} | all-to-all | bytes 1048576 | tf_op jit(solution)/shard_map/all_to_all | solution.py:255
  79.4 0.8 %copy.9 = bf16[16,8,8,256]{3,2,0,1:T(8,128)(2,1)} copy(bf16[16,8,8,256]{3,2,1,0:T(8,128)(2,1)S(1)} %bitcast.31) | data formatting | bytes 1048576 | tf_op jit(solution)/shard_map/reshape | solution.py:295
  (9 shorter events, 0.2 us)
Async XLA Ops:
  0.0 17.9 %copy-start.1 = (bf16[64,4096]{1,0:T(8,128)(2,1)S(1)}, bf16[64,4096]{1,0:T(8,128)(2,1)}, u32[]{:S(2)}) copy-start(bf16[64,4096]{1,0:T(8,128)(2,1)} %param.4) | copy-start | bytes 1572868
  14.4 9.7 %collective-permute-start = (bf16[1024,128]{1,0:T(8,128)(2,1)S(1)}, bf16[1024,128]{1,0:T(8,128)(2,1)S(1)}, u32[]{:S(2)}, u32[]{:S(2)}) collective-permute-start(bf16[1024,128]{1,0:T(8,128)(2,1)S(1)} %bitcast.25), channel_id=1, source_target_pairs={{0,32},{1,33},{2,34},{3,35},{4,36},{5,37},{6,38},{7,39},{8,40},{9,... | collective-permute-start | bytes 786440 | tf_op jit(solution)/shard_map/ppermute | solution.py:266
  18.8 22.9 %copy-start = (s32[16]{0:T(128)S(1)}, s32[16]{0:T(128)}, u32[]{:S(2)}) copy-start(s32[16]{0:T(128)} %starts.3) | copy-start | bytes 196
  18.8 15.1 %all-to-all-start.1 = ((bf16[16,64,256]{2,1,0:T(8,128)(2,1)}), bf16[16,64,256]{2,1,0:T(8,128)(2,1)S(1)}, u32[]{:S(2)}, u32[]{:S(2)}) async-start(bf16[16,64,256]{2,1,0:T(8,128)(2,1)} %bitcast.24), calls=%async_computation.1 | async-start | bytes 1048576 | tf_op jit(solution)/shard_map/all_to_all | solution.py:255
  24.1 10.1 %collective-permute-start.1 = (bf16[1024,128]{1,0:T(8,128)(2,1)S(1)}, bf16[1024,128]{1,0:T(8,128)(2,1)S(1)}, u32[]{:S(2)}, u32[]{:S(2)}) collective-permute-start(bf16[1024,128]{1,0:T(8,128)(2,1)S(1)} %collective-permute-done.refs_1_), channel_id=1, source_target_pairs={{32,64},{33,65},{34,66},{35,67},{36,68},{37,69},{38,70},{39,71},{4... | collective-permute-start | bytes 786440 | tf_op jit(solution)/shard_map/ppermute | solution.py:266
  28.9 9.1 %collective-permute-start.2 = (bf16[1024,128]{1,0:T(8,128)(2,1)S(1)}, bf16[1024,128]{1,0:T(8,128)(2,1)S(1)}, u32[]{:S(2)}, u32[]{:S(2)}) collective-permute-start(bf16[1024,128]{1,0:T(8,128)(2,1)S(1)} %collective-permute-done.refs_1_), channel_id=1, source_target_pairs={{0,24},{1,25},{2,26},{3,27},{4,28},{5,29},{6,30},{7,31},{8,16},{9,... | collective-permute-start | bytes 786440 | tf_op jit(solution)/shard_map/ppermute | solution.py:266
  31.0 10.6 %collective-permute-start.4 = (bf16[2048,128]{1,0:T(8,128)(2,1)S(1)}, bf16[2048,128]{1,0:T(8,128)(2,1)S(1)}, u32[]{:S(2)}, u32[]{:S(2)}) collective-permute-start(bf16[2048,128]{1,0:T(8,128)(2,1)S(1)} %pad_maximum_fusion), channel_id=1, source_target_pairs={{0,1},{1,0},{2,3},{3,2},{4,5},{5,4},{6,7},{7,6},{8,9},{9,8},{10,11... | collective-permute-start | bytes 1572872 | tf_op jit(solution)/shard_map/ppermute | solution.py:266
  34.2 15.7 %collective-permute-start.3 = (bf16[1024,128]{1,0:T(8,128)(2,1)S(1)}, bf16[1024,128]{1,0:T(8,128)(2,1)S(1)}, u32[]{:S(2)}, u32[]{:S(2)}) collective-permute-start(bf16[1024,128]{1,0:T(8,128)(2,1)S(1)} %broadcast_select_fusion), channel_id=1, source_target_pairs={{0,24},{1,25},{2,26},{3,27},{4,28},{5,29},{6,30},{7,31},{8,16},{9,... | collective-permute-start | bytes 786440 | tf_op jit(solution)/shard_map/ppermute | solution.py:266
  38.0 13.9 %collective-permute-start.5 = (bf16[2048,128]{1,0:T(8,128)(2,1)S(1)}, bf16[2048,128]{1,0:T(8,128)(2,1)S(1)}, u32[]{:S(2)}, u32[]{:S(2)}) collective-permute-start(bf16[2048,128]{1,0:T(8,128)(2,1)S(1)} %pad_maximum_fusion.1), channel_id=1, source_target_pairs={{0,1},{1,0},{2,3},{3,2},{4,5},{5,4},{6,7},{7,6},{8,9},{9,8},{10,11... | collective-permute-start | bytes 1572872 | tf_op jit(solution)/shard_map/ppermute | solution.py:266
  50.0 3.4 %collective-permute-start.6 = (bf16[1024,128]{1,0:T(8,128)(2,1)S(1)}, bf16[1024,128]{1,0:T(8,128)(2,1)S(1)}, u32[]{:S(2)}, u32[]{:S(2)}) collective-permute-start(bf16[1024,128]{1,0:T(8,128)(2,1)S(1)} %collective-permute-done.3.refs_2_), channel_id=1, source_target_pairs={{0,1},{1,0},{2,3},{3,2},{4,5},{5,4},{6,7},{7,6},{8,9},{9,8},{10,11... | collective-permute-start | bytes 786440 | tf_op jit(solution)/shard_map/ppermute | solution.py:266

commit v2 on v1

--- a/solution.py
+++ b/solution.py
@@ -18,6 +18,7 @@
 FLOOR = -1.0e30
 SCALE = D_HEAD**-0.5 * math.log2(math.e)
 PART = 128
+PIECE = BLOCK // 2
 ROWS = 2 * BLOCK
 
 
@@ -104,6 +105,13 @@
     groups = [slice(g, g + D_HEAD) for g in range(0, BLOCK, D_HEAD)]
     parts = [slice(r, r + PART) for r in range(0, ROWS, PART)]
 
+    def pieces(half):
+        for i in range(4):
+            part, head = divmod(i, 2)
+            first = half * BLOCK + part * PIECE
+            yield (slice(i * PIECE, (i + 1) * PIECE), slice(first, first + PIECE),
+                   slice(head * D_HEAD, (head + 1) * D_HEAD))
+
     class Tile:
         def __init__(self, half):
             self.half = half
@@ -114,11 +122,10 @@
             border = jnp.where(pos == 0, lasts[0], lasts[1]) - s_first - pos * BLOCK
             column = jnp.where(row >= border, pos + 2, pos)
             marks = jnp.where((lane == pos) | (lane == column), 1.0, 0.0).astype(jnp.bfloat16)
-            for head in range(2):
-                to = slice(head * BLOCK, (head + 1) * BLOCK)
-                at = slice(head * D_HEAD, (head + 1) * D_HEAD)
-                qx_ref[half, to, 0:D_HEAD] = q_ref[half * BLOCK:(half + 1) * BLOCK, at]
-                qx_ref[half, to, D_HEAD:] = marks
+            for rows, tokens, columns in pieces(half):
+                qx_ref[half, rows, 0:D_HEAD] = q_ref[tokens, columns]
+                query = tokens.start % BLOCK
+                qx_ref[half, rows, D_HEAD:] = marks[query:query + PIECE]
             m = n - pos
             if late:
                 self.steps = jnp.clip(m, 0, 2) + jnp.clip(m - 4, 0, 4)
@@ -128,41 +135,84 @@
                 self.steps = beside + jnp.clip(m - 2, 0, 2)
                 self.distance = lambda i: jnp.where((pos == 1) & (i == 0), 1, i + 3)
 
-        def keys(self, d):
-            return pl.ds(pl.multiple_of((self.own - d) * BLOCK, BLOCK), BLOCK)
-
-        def weigh(self, b, d):
+        def keys(self, d, first=0, size=BLOCK):
+            return pl.ds(pl.multiple_of((self.own - d) * BLOCK + first, PIECE), size)
+
+        def score(self, d, rows=slice(None), first=0, size=BLOCK):
+            return lax.dot_general(
+                qx_ref[self.half, rows], k_ref[self.keys(d, first, size), :],
+                (((1,), (1,)), ((), ())), preferred_element_type=jnp.float32)
+
+        def mix(self, d, rows=slice(None), first=0, size=BLOCK, at=0):
+            return jnp.dot(weights[rows, at + first:at + first + size],
+                           v_ref[self.keys(d, first, size), :], preferred_element_type=jnp.float32)
+
+        def exponents(self, b, at=0, diagonal=False):
             for r in parts:
                 for g in groups:
+                    if diagonal and r.start < BLOCK and g.start >= PIECE:
+                        continue
                     p = jnp.exp2(self.scores[b, r, g] * SCALE - shift[r, :])
-                    weights[r, g] = p.astype(jnp.bfloat16)
-            return jnp.dot(weights[...], v_ref[self.keys(d), :], preferred_element_type=jnp.float32)
-
-        def fresh(self, b, d):
-            self.scores[b] = lax.dot_general(
-                qx_ref[self.half], k_ref[self.keys(d), :], (((1,), (1,)), ((), ())),
-                preferred_element_type=jnp.float32)
+                    weights[r, at + g.start:at + g.stop] = p.astype(jnp.bfloat16)
+
+        def tops(self, blocks, diagonal=False):
             for r in parts:
                 top = top_ref[r, :]
-                query = slice(r.start % BLOCK, r.start % BLOCK + PART)
-                for g in groups:
-                    part = self.scores[b, r, g]
-                    if isinstance(d, int):
-                        part = jnp.where(lane[query] + g.start <= row[query], part, FLOOR)
-                        self.scores[b, r, g] = part
-                    top = jnp.maximum(top, part)
+                query = r.start // BLOCK * PIECE + r.start % PIECE
+                query = slice(query, query + PART)
+                for b in blocks:
+                    for g in groups:
+                        if diagonal and r.start < BLOCK and g.start >= PIECE:
+                            continue
+                        part = self.scores[b, r, g]
+                        if diagonal:
+                            part = jnp.where(lane[query] + g.start <= row[query], part, FLOOR)
+                            self.scores[b, r, g] = part
+                        top = jnp.maximum(top, part)
                 top_ref[r, :] = top
 
+        def weigh(self, i, blocks):
+            for j in range(blocks):
+                self.exponents(i + j if late else i + j + 1, j * BLOCK)
+            product = self.mix(self.distance(i))
+            for j in range(1, blocks):
+                product += self.mix(self.distance(i + j), at=j * BLOCK)
+            acc[...] += product
+
+        def fresh(self, i, blocks):
+            buffers = [i + j if late else i + j + 1 for j in range(blocks)]
+            for j in range(blocks):
+                self.scores[buffers[j]] = self.score(self.distance(i + j))
+            self.tops(buffers)
+
+        def weigh_own(self):
+            self.exponents(0, diagonal=True)
+            acc[...] = self.mix(0, size=PIECE)
+            acc[BLOCK:, :] += self.mix(0, rows=slice(BLOCK, ROWS), first=PIECE, size=PIECE)
+
+        def fresh_own(self):
+            self.scores[0, :, 0:PIECE] = self.score(0, size=PIECE)
+            self.scores[0, BLOCK:, PIECE:] = self.score(0, slice(BLOCK, ROWS), PIECE, PIECE)
+            self.tops([0], diagonal=True)
+
     def loop(first, stop, old, young):
-        def go(i, carry):
-            b = i if late else i + 1
+        def go(i, blocks):
             if old:
-                acc[...] += old.weigh(b, old.distance(i))
+                old.weigh(i, blocks)
             if young:
-                young.fresh(b, young.distance(i))
+                young.fresh(i, blocks)
+
+        def two(i, carry):
+            go(first + 2 * i, 2)
             return carry
 
-        lax.fori_loop(first, stop, go, 0)
+        def one(i, carry):
+            go(i, 1)
+            return carry
+
+        twos = (stop - first) // 2
+        lax.fori_loop(0, twos, two, 0)
+        lax.fori_loop(first + 2 * twos, stop, one, 0)
 
     tiles = [Tile(half) for half in range(2)]
     for low, high in ranges:
@@ -171,12 +221,12 @@
         cur = tiles[t - 1] if t > 0 else None
         new = tiles[t] if t < 2 else None
         if cur and not late:
-            acc[...] = cur.weigh(0, 0)
+            cur.weigh_own()
         if new and late:
             top_ref[...] = top_in[new.half]
         elif new:
             top_ref[...] = jnp.full((ROWS, D_HEAD), FLOOR, jnp.float32)
-            new.fresh(0, 0)
+            new.fresh_own()
         if cur and new:
             both = jnp.minimum(cur.steps, new.steps)
             loop(0, both, cur, new)
@@ -187,11 +237,9 @@
         else:
             loop(0, new.steps, None, new)
         if cur and late:
-            for head in range(2):
-                r = slice(head * BLOCK, (head + 1) * BLOCK)
-                mixed = acc[r, 0:D_HEAD] / acc[r, D_HEAD:]
-                out_ref[cur.half * BLOCK:(cur.half + 1) * BLOCK,
-                        head * D_HEAD:(head + 1) * D_HEAD] = mixed.astype(jnp.bfloat16)
+            for rows, tokens, columns in pieces(cur.half):
+                mixed = acc[rows, 0:D_HEAD] / acc[rows, D_HEAD:]
+                out_ref[tokens, columns] = mixed.astype(jnp.bfloat16)
         elif cur:
             acc_out[cur.half] = acc[...]
         if new:
@@ -205,6 +253,17 @@
                     acc[r, D_HEAD:] = acc_in[new.half, r, D_HEAD:] * rescale
                 else:
                     top_out[new.half, r, :] = top
+
+
+def pack(keys, values, out, sems):
+    copies = []
+    for i in range(out.shape[0]):
+        head, part = divmod(i, 2)
+        source = (keys, values)[part].at[:, head * D_HEAD:(head + 1) * D_HEAD]
+        copies.append(pltpu.make_async_copy(source, out.at[i], sems.at[i]))
+        copies[-1].start()
+    for copy in copies:
+        copy.wait()
 
 
 def attention(late, doc_starts, q, blocks, state=()):
@@ -228,14 +287,14 @@
             pltpu.VMEM((2, ROWS, 2 * D_HEAD), jnp.bfloat16),
             scores,
             scores,
-            pltpu.VMEM((ROWS, BLOCK), jnp.bfloat16),
+            pltpu.VMEM((ROWS, 2 * BLOCK), jnp.bfloat16),
             pltpu.VMEM((ROWS, 2 * D_HEAD), jnp.float32),
             pltpu.VMEM((ROWS, D_HEAD), jnp.float32),
             pltpu.VMEM((ROWS, D_HEAD), jnp.float32),
             pltpu.SemaphoreType.DMA((SLOTS,)),
             pltpu.SemaphoreType.DMA((SLOTS,)),
         ],
-        compiler_params=pltpu.CompilerParams(vmem_limit_bytes=44 * 1024 * 1024),
+        compiler_params=pltpu.CompilerParams(vmem_limit_bytes=(44 if late else 36) * 1024 * 1024),
         cost_estimate=pl.CostEstimate(
             flops=(3 if late else 2) * 10**9, bytes_accessed=4 * 10**6, transcendentals=3 * 10**6
         ),
@@ -272,9 +331,15 @@
         return move(x, lambda d, z, y: d ^ 1)
 
     heads = keys.shape[1] // D_HEAD
-    kv = jnp.stack(
-        [keys.reshape(rows, heads, D_HEAD), values.reshape(rows, heads, D_HEAD)], axis=2
-    ).reshape(rows, 2 * heads, D_HEAD).transpose(1, 0, 2)
+    kv = pl.pallas_call(
+        pack,
+        out_shape=jax.ShapeDtypeStruct((2 * heads, rows, D_HEAD), keys.dtype),
+        in_specs=[pl.BlockSpec(memory_space=pl.ANY)] * 2,
+        out_specs=pl.BlockSpec(memory_space=pltpu.VMEM),
+        scratch_shapes=[pltpu.SemaphoreType.DMA((2 * heads,))],
+        compiler_params=pltpu.CompilerParams(vmem_limit_bytes=60 * 1024 * 1024),
+        name="pack",
+    )(keys, values)
     own = exchange(kv).reshape(SUPER, D_HEAD)
     q = queries.reshape(rows, 2 * heads, 2 * D_HEAD).transpose(1, 0, 2)
     q = exchange(q).reshape(SUPER, 2 * D_HEAD)

time: 80.7 us -> 81.1 us (level)
  the two profiles are of different devices: /device:TPU:209 before, /device:TPU:113 now
where the time goes in v2:
time: 81.1 us; the launch traced here: 80.5 us
  starting transfers between devices  27.7 us (34%)
  blocking collectives  27.6 us (34%)
  Pallas kernels  20.5 us (25%)
  local copies, waits for them, and re-layouts  2.72 us (3%)
  waiting for transfers between devices  1.72 us (2%)
    all_to_all x2, blocking collectives, exchange(): lax.all_to_all(x, 'd', split_axis=0, concat_axis=0, axis_index_groups=gro...  27.6 us
    ppermute x7, starting transfers between devices, move(): return lax.ppermute(x, 'd', pairs)  22.4 us
    pallas_call x2, Pallas kernels, attention(): pl.pallas_call(functools.partial(attend, late), out_shape=out_shape, in_s...  18.8 us
    all_to_all x1, starting transfers between devices, exchange(): lax.all_to_all(x, 'd', split_axis=0, concat_axis=0, axis_index_groups=gro...  5.32 us
    reshape x1, local copies, waits for them, and re-layouts, per_device(): q = queries.reshape(rows, 2 * heads, 2 * D_HEAD).transpose(1, 0, 2)  1.89 us
    pallas_call x1, Pallas kernels, per_device(): pl.pallas_call(pack, out_shape=jax.ShapeDtypeStruct((2 * heads, rows, D_H...  1.74 us
  transfers between devices with their start and end apart: 8, of which 2 were waited for; matrix products, arithmetic and copies ran while one was open for 3% of the time, Pallas kernels for 10%

profile of v2, /device:TPU:113, one launch (start us, length us, event | category | flops | bytes accessed | tf_op | source)
XLA Modules:
  0.0 80.5 jit_solution(13627596787921537515)
XLA Ops:
  0.0 1.7 %pack.1 = bf16[16,64,128]{2,1,0:T(8,128)(2,1)} custom-call(bf16[64,1024]{1,0:T(8,128)(2,1)} %keys.1, bf16[64,1024]{1,0:T(8,128)(2,1)} %values.1), custom_call_target="tpu_custom_call" | custom-call | tf_op jit(solution)/shard_map/pack/pallas_call | solution.py:334
  1.7 12.6 %all_to_all.15 = bf16[16,64,128]{2,1,0:T(8,128)(2,1)S(1)} all-to-all(bf16[16,64,128]{2,1,0:T(8,128)(2,1)} %pack.1), channel_id=1, replica_groups={{0,1,2,3,4,5,6,7,8,9,10,11,12,13,14,15},{24,25,26,27,28,29,30,31,16,17,..., dimensions={0} | all-to-all | bytes 524288 | tf_op jit(solution)/shard_map/all_to_all | solution.py:314
  14.3 4.7 %collective-permute-start = (bf16[1024,128]{1,0:T(8,128)(2,1)S(1)}, bf16[1024,128]{1,0:T(8,128)(2,1)S(1)}, u32[]{:S(2)}, u32[]{:S(2)}) collective-permute-start(bf16[1024,128]{1,0:T(8,128)(2,1)S(1)} %bitcast.14), channel_id=1, source_target_pairs={{0,32},{1,33},{2,34},{3,35},{4,36},{5,37},{6,38},{7,39},{8,40},{9,... | collective-permute-start | bytes 786440 | tf_op jit(solution)/shard_map/ppermute | solution.py:325
  19.1 1.9 %copy.10 = bf16[8,16,8,256]{3,2,0,1:T(8,128)(2,1)} copy(bf16[8,16,8,256]{3,2,1,0:T(8,128)(2,1)} %bitcast.21) | data formatting | bytes 1048576 | tf_op jit(solution)/shard_map/reshape | solution.py:344
  21.0 5.3 %all-to-all-start.1 = ((bf16[16,64,256]{2,1,0:T(8,128)(2,1)}), bf16[16,64,256]{2,1,0:T(8,128)(2,1)S(1)}, u32[]{:S(2)}, u32[]{:S(2)}) async-start(bf16[16,64,256]{2,1,0:T(8,128)(2,1)} %bitcast.13), calls=%async_computation.1 | async-start | bytes 1048576 | tf_op jit(solution)/shard_map/all_to_all | solution.py:314
  26.3 0.0 collective-permute-done.refs_1_
  26.3 3.5 %collective-permute-start.1 = (bf16[1024,128]{1,0:T(8,128)(2,1)S(1)}, bf16[1024,128]{1,0:T(8,128)(2,1)S(1)}, u32[]{:S(2)}, u32[]{:S(2)}) collective-permute-start(bf16[1024,128]{1,0:T(8,128)(2,1)S(1)} %collective-permute-done.refs_1_), channel_id=1, source_target_pairs={{32,64},{33,65},{34,66},{35,67},{36,68},{37,69},{38,70},{39,71},{4... | collective-permute-start | bytes 786440 | tf_op jit(solution)/shard_map/ppermute | solution.py:325
  29.8 2.1 %collective-permute-start.2 = (bf16[1024,128]{1,0:T(8,128)(2,1)S(1)}, bf16[1024,128]{1,0:T(8,128)(2,1)S(1)}, u32[]{:S(2)}, u32[]{:S(2)}) collective-permute-start(bf16[1024,128]{1,0:T(8,128)(2,1)S(1)} %collective-permute-done.refs_1_), channel_id=1, source_target_pairs={{0,24},{1,25},{2,26},{3,27},{4,28},{5,29},{6,30},{7,31},{8,16},{9,... | collective-permute-start | bytes 786440 | tf_op jit(solution)/shard_map/ppermute | solution.py:325
  32.0 3.5 %collective-permute-start.4 = (bf16[2048,128]{1,0:T(8,128)(2,1)S(1)}, bf16[2048,128]{1,0:T(8,128)(2,1)S(1)}, u32[]{:S(2)}, u32[]{:S(2)}) collective-permute-start(bf16[2048,128]{1,0:T(8,128)(2,1)S(1)} %pad_maximum_fusion), channel_id=1, source_target_pairs={{0,1},{1,0},{2,3},{3,2},{4,5},{5,4},{6,7},{7,6},{8,9},{9,8},{10,11... | collective-permute-start | bytes 1572872 | tf_op jit(solution)/shard_map/ppermute | solution.py:325
  35.5 0.2 all-to-all-done.1
  35.7 0.0 collective-permute-done.1.refs_0_
  35.7 0.1 broadcast_select_fusion
  35.8 3.0 %collective-permute-start.3 = (bf16[1024,128]{1,0:T(8,128)(2,1)S(1)}, bf16[1024,128]{1,0:T(8,128)(2,1)S(1)}, u32[]{:S(2)}, u32[]{:S(2)}) collective-permute-start(bf16[1024,128]{1,0:T(8,128)(2,1)S(1)} %broadcast_select_fusion), channel_id=1, source_target_pairs={{0,24},{1,25},{2,26},{3,27},{4,28},{5,29},{6,30},{7,31},{8,16},{9,... | collective-permute-start | bytes 786440 | tf_op jit(solution)/shard_map/ppermute | solution.py:325
  38.8 0.0 collective-permute-done.2.refs_1_
  38.8 3.6 %collective-permute-start.5 = (bf16[2048,128]{1,0:T(8,128)(2,1)S(1)}, bf16[2048,128]{1,0:T(8,128)(2,1)S(1)}, u32[]{:S(2)}, u32[]{:S(2)}) collective-permute-start(bf16[2048,128]{1,0:T(8,128)(2,1)S(1)} %pad_maximum_fusion.1), channel_id=1, source_target_pairs={{0,1},{1,0},{2,3},{3,2},{4,5},{5,4},{6,7},{7,6},{8,9},{9,8},{10,11... | collective-permute-start | bytes 1572872 | tf_op jit(solution)/shard_map/ppermute | solution.py:325
  42.4 0.0 collective-permute-done.4.refs_2_
  42.4 7.8 %early_blocks.1 = (f32[2,1024,256]{2,1,0:T(8,128)S(1)}, f32[2,1024,128]{2,1,0:T(8,128)S(1)}) custom-call(s32[16]{0:T(128)S(1)} %copy-done, bf16[1024,256]{1,0:T(8,128)(2,1)S(1)} %bitcast.17, bf16[1024,128]{1,0:T(8,128)(2,1)S(1)} %bitcast.16, bf16[1024,128]{1,0:T(8,128)(2,1)S(1)} %collective-permute-done.refs_1_, ...), custom_call_target="tpu_custom_call" | custom-call | flops 2000000000 | bytes 4000000 | tf_op jit(solution)/shard_map/early_blocks/pallas_call | solution.py:278
  50.2 0.0 collective-permute-done.3.refs_2_
  50.3 1.9 %collective-permute-start.6 = (bf16[1024,128]{1,0:T(8,128)(2,1)S(1)}, bf16[1024,128]{1,0:T(8,128)(2,1)S(1)}, u32[]{:S(2)}, u32[]{:S(2)}) collective-permute-start(bf16[1024,128]{1,0:T(8,128)(2,1)S(1)} %collective-permute-done.3.refs_2_), channel_id=1, source_target_pairs={{0,1},{1,0},{2,3},{3,2},{4,5},{5,4},{6,7},{7,6},{8,9},{9,8},{10,11... | collective-permute-start | bytes 786440 | tf_op jit(solution)/shard_map/ppermute | solution.py:325
  52.2 0.0 collective-permute-done.5.refs_3_
  52.2 1.5 %collective-permute-done.6.refs_4_ = bf16[1024,128]{1,0:T(8,128)(2,1)S(1)} collective-permute-done((bf16[1024,128]{1,0:T(8,128)(2,1)S(1)}, bf16[1024,128]{1,0:T(8,128)(2,1)S(1)}, u32[]{:S(2)}, u32[]{:S(2)}) %collective-permute-start.6) | collective-permute-done | bytes 262176 | tf_op jit(solution)/shard_map/ppermute | solution.py:325
  53.7 11.0 %late_blocks.1 = bf16[1024,256]{1,0:T(8,128)(2,1)S(1)} custom-call(s32[16]{0:T(128)S(1)} %copy-done, bf16[1024,256]{1,0:T(8,128)(2,1)S(1)} %bitcast.18, bf16[1024,128]{1,0:T(8,128)(2,1)S(1)} %collective-permute-done.1.refs_0_, bf16[1024,128]{1,0:T(8,128)(2,1)S(1)} %collective-permute-done.2.refs_1_, bf16[1024,128]{1,0:T(8,128)(2,1)S(1)} %collective-permute-done.3.refs_2_, ...), custom_call_target="tpu_custom_call" | custom-call | flops 3000000000 | bytes 4000000 | tf_op jit(solution)/shard_map/late_blocks/pallas_call | solution.py:278
  64.7 15.0 %all_to_all.16 = bf16[16,64,256]{2,1,0:T(8,128)(2,1)S(1)} all-to-all(bf16[16,64,256]{2,1,0:T(8,128)(2,1)S(1)} %bitcast.19), channel_id=1, replica_groups={{0,1,2,3,4,5,6,7,8,9,10,11,12,13,14,15},{24,25,26,27,28,29,30,31,16,17,..., dimensions={0} | all-to-all | bytes 1048576 | tf_op jit(solution)/shard_map/all_to_all | solution.py:314
  79.7 0.8 %copy.8 = bf16[16,8,8,256]{3,2,0,1:T(8,128)(2,1)} copy(bf16[16,8,8,256]{3,2,1,0:T(8,128)(2,1)S(1)} %bitcast.20) | data formatting | bytes 1048576 | tf_op jit(solution)/shard_map/reshape | solution.py:360
  (4 shorter events, 0.1 us)
Async XLA Ops:
  14.3 12.0 %collective-permute-start = (bf16[1024,128]{1,0:T(8,128)(2,1)S(1)}, bf16[1024,128]{1,0:T(8,128)(2,1)S(1)}, u32[]{:S(2)}, u32[]{:S(2)}) collective-permute-start(bf16[1024,128]{1,0:T(8,128)(2,1)S(1)} %bitcast.14), channel_id=1, source_target_pairs={{0,32},{1,33},{2,34},{3,35},{4,36},{5,37},{6,38},{7,39},{8,40},{9,... | collective-permute-start | bytes 786440 | tf_op jit(solution)/shard_map/ppermute | solution.py:325
  21.0 21.5 %copy-start = (s32[16]{0:T(128)S(1)}, s32[16]{0:T(128)}, u32[]{:S(2)}) copy-start(s32[16]{0:T(128)} %starts.3) | copy-start | bytes 196
  21.0 14.7 %all-to-all-start.1 = ((bf16[16,64,256]{2,1,0:T(8,128)(2,1)}), bf16[16,64,256]{2,1,0:T(8,128)(2,1)S(1)}, u32[]{:S(2)}, u32[]{:S(2)}) async-start(bf16[16,64,256]{2,1,0:T(8,128)(2,1)} %bitcast.13), calls=%async_computation.1 | async-start | bytes 1048576 | tf_op jit(solution)/shard_map/all_to_all | solution.py:314
  26.3 9.4 %collective-permute-start.1 = (bf16[1024,128]{1,0:T(8,128)(2,1)S(1)}, bf16[1024,128]{1,0:T(8,128)(2,1)S(1)}, u32[]{:S(2)}, u32[]{:S(2)}) collective-permute-start(bf16[1024,128]{1,0:T(8,128)(2,1)S(1)} %collective-permute-done.refs_1_), channel_id=1, source_target_pairs={{32,64},{33,65},{34,66},{35,67},{36,68},{37,69},{38,70},{39,71},{4... | collective-permute-start | bytes 786440 | tf_op jit(solution)/shard_map/ppermute | solution.py:325
  29.8 8.9 %collective-permute-start.2 = (bf16[1024,128]{1,0:T(8,128)(2,1)S(1)}, bf16[1024,128]{1,0:T(8,128)(2,1)S(1)}, u32[]{:S(2)}, u32[]{:S(2)}) collective-permute-start(bf16[1024,128]{1,0:T(8,128)(2,1)S(1)} %collective-permute-done.refs_1_), channel_id=1, source_target_pairs={{0,24},{1,25},{2,26},{3,27},{4,28},{5,29},{6,30},{7,31},{8,16},{9,... | collective-permute-start | bytes 786440 | tf_op jit(solution)/shard_map/ppermute | solution.py:325
  32.0 10.4 %collective-permute-start.4 = (bf16[2048,128]{1,0:T(8,128)(2,1)S(1)}, bf16[2048,128]{1,0:T(8,128)(2,1)S(1)}, u32[]{:S(2)}, u32[]{:S(2)}) collective-permute-start(bf16[2048,128]{1,0:T(8,128)(2,1)S(1)} %pad_maximum_fusion), channel_id=1, source_target_pairs={{0,1},{1,0},{2,3},{3,2},{4,5},{5,4},{6,7},{7,6},{8,9},{9,8},{10,11... | collective-permute-start | bytes 1572872 | tf_op jit(solution)/shard_map/ppermute | solution.py:325
  35.8 14.5 %collective-permute-start.3 = (bf16[1024,128]{1,0:T(8,128)(2,1)S(1)}, bf16[1024,128]{1,0:T(8,128)(2,1)S(1)}, u32[]{:S(2)}, u32[]{:S(2)}) collective-permute-start(bf16[1024,128]{1,0:T(8,128)(2,1)S(1)} %broadcast_select_fusion), channel_id=1, source_target_pairs={{0,24},{1,25},{2,26},{3,27},{4,28},{5,29},{6,30},{7,31},{8,16},{9,... | collective-permute-start | bytes 786440 | tf_op jit(solution)/shard_map/ppermute | solution.py:325
  38.8 13.3 %collective-permute-start.5 = (bf16[2048,128]{1,0:T(8,128)(2,1)S(1)}, bf16[2048,128]{1,0:T(8,128)(2,1)S(1)}, u32[]{:S(2)}, u32[]{:S(2)}) collective-permute-start(bf16[2048,128]{1,0:T(8,128)(2,1)S(1)} %pad_maximum_fusion.1), channel_id=1, source_target_pairs={{0,1},{1,0},{2,3},{3,2},{4,5},{5,4},{6,7},{7,6},{8,9},{9,8},{10,11... | collective-permute-start | bytes 1572872 | tf_op jit(solution)/shard_map/ppermute | solution.py:325
  50.3 3.4 %collective-permute-start.6 = (bf16[1024,128]{1,0:T(8,128)(2,1)S(1)}, bf16[1024,128]{1,0:T(8,128)(2,1)S(1)}, u32[]{:S(2)}, u32[]{:S(2)}) collective-permute-start(bf16[1024,128]{1,0:T(8,128)(2,1)S(1)} %collective-permute-done.3.refs_2_), channel_id=1, source_target_pairs={{0,1},{1,0},{2,3},{3,2},{4,5},{5,4},{6,7},{7,6},{8,9},{9,8},{10,11... | collective-permute-start | bytes 786440 | tf_op jit(solution)/shard_map/ppermute | solution.py:325
